TPU v7x, 256 devices: a whole 4x4x8 slice. The times are simulated.
256 devices in a mesh: dp: 8 (over z), seq: 32 (over y, x, core).
Axes of the slice: x: 4, y: 4, z: 8, core: 2. Of those that a mesh axis runs over, the one named last changes fastest.
Arguments:
- gate_input: bfloat16 [8, 4096, 4096], P('dp', 'seq'), may hold values from -6 to 6
- conv_input: bfloat16 [8, 4096, 4096], P('dp', 'seq'), may hold values from -6 to 6
- grad_output: bfloat16 [8, 4096, 4096], P('dp', 'seq'), may hold values from -6 to 6
- filter_taps: bfloat16 [4096, 4096], P('seq'), may hold values from -0.09375 to 0.09375
- block_order: int32 [32], replicated, may hold values from 0 to 31, each once
- owner_rows: int32 [8, 4096], P('dp', 'seq'), may hold values from 0 to 31, as said below
Outputs:
- grad_gate: bfloat16 [8, 4096, 4096], P('dp', 'seq')
- grad_returned: bfloat16 [8, 8192, 4096], P('dp', 'seq')
- grad_filter: float32 [4096, 4096], P('dp', 'seq')
Inputs may be any that keep to these rules, and one draw needn't show every extreme that they name: `owner_rows`: in each sequence, no owner is named by more than 8 of the 128 rows of one block, and one owner is named by exactly 8 rows of every block, so that it receives 256 rows. `block_order`: each block number appears once.
All inputs are finite; a program needn't handle non-finite values.
Results may differ from a plain program's by a relative error of at most 0.019.
Values may be sent and summed in bfloat16 or wider, within the bound.
A program may use at most 128 MiB of HBM per device.

v0:
```python
import functools
import math

import jax
import jax.numpy as jnp
import numpy as np
from jax import lax
from jax.experimental import pallas as pl
from jax.experimental.pallas import tpu as pltpu
from jax.sharding import PartitionSpec as P

F32, BF16, I32 = jnp.float32, jnp.bfloat16, jnp.int32
MESH = pl.DeviceIdType.MESH
VMEM_BYTES = 60 * 2**20


def spectrum_of(values):
    n = len(values)
    if n == 1:
        return [(values[0], None)]
    even, odd = spectrum_of(values[0::2]), spectrum_of(values[1::2])
    result = [None] * n
    for k in range(n // 2):
        angle = math.pi * (2 * k + 1) / (2 * n)
        c, s = math.cos(angle), -math.sin(angle)
        (er, ei), (hr, hi) = even[k], odd[k]
        if ei is None:
            tr, ti = c * hr, s * hr
            result[k], result[n - 1 - k] = (er + tr, ti), (er - tr, ti)
            continue
        tr, ti = c * hr - s * hi, c * hi + s * hr
        result[k], result[n - 1 - k] = (er + tr, ei + ti), (er - tr, ti - ei)
    return result


def values_of(spectrum):
    n = len(spectrum)
    if n == 1:
        return [spectrum[0][0]]
    even, odd = [], []
    for k in range(n // 2):
        angle = math.pi * (2 * k + 1) / (2 * n)
        c, s = math.cos(angle), math.sin(angle)
        (zr, zi), (pr, pi) = spectrum[k], spectrum[n - 1 - k]
        dr, di = zr - pr, zi + pi
        even.append((zr + pr, zi - pi))
        odd.append((c * dr - s * di, c * di + s * dr))
    result = [None] * n
    result[0::2], result[1::2] = values_of(even), values_of(odd)
    return result


@functools.lru_cache
def tables(blocks, rows):
    k1 = np.arange(blocks)[:, None, None]
    k2 = np.arange(rows)[None, :, None]
    n1 = np.arange(rows)[None, None, :]
    length = 2 * blocks * rows
    phase = (np.pi / length) * ((2 * k1 + 1) * n1 + 2 * blocks * 2 * (k2 * n1 % rows))
    c, s = np.cos(phase), np.sin(phase)
    table = np.concatenate([np.concatenate([c, s], 2), np.concatenate([-s, c], 2)], 1)
    back = np.swapaxes(table, 1, 2) / (blocks * rows)
    return table.astype(jnp.bfloat16), back.astype(jnp.bfloat16)


def kernel(
    n_dp,
    n_seq,
    order,
    place_of,
    owners_in,
    gate,
    conv,
    upstream,
    taps,
    table_in,
    back_in,
    sig_out,
    rows_out,
    parts_out,
    gate_v,
    up_v,
    mixed_v,
    own_got,
    conv_got,
    taps_got,
    mixed_got,
    table,
    back_table,
    pair_a,
    mixed_a,
    specs,
    turned,
    sig_time,
    sig_send,
    back_time,
    starts,
    packed,
    rows_send,
    filt_send,
    send_sem,
    recv_sem,
    local_sem,
):
    dp, seq = lax.axis_index("dp"), lax.axis_index("seq")
    rows = gate_v.shape[0]
    lanes = conv_got.shape[2]
    tile = 16
    slot = rows_send.shape[1] // n_seq

    loads = [
        pltpu.make_async_copy(a, b, local_sem.at[i])
        for i, (a, b) in enumerate(
            ((gate, gate_v), (upstream, up_v), (table_in, table), (back_in, back_table))
        )
    ]
    for load in loads:
        load.start()

    barrier = pltpu.get_barrier_semaphore()

    @pl.loop(1, n_seq)
    def _(hop):
        to = lax.rem(seq + hop, n_seq)
        pl.semaphore_signal(barrier, inc=1, device_id=(dp, to), device_id_type=MESH)

    @pl.loop(1, n_dp)
    def _(hop):
        to = lax.rem(dp + hop, n_dp)
        pl.semaphore_signal(barrier, inc=1, device_id=(to, seq), device_id_type=MESH)

    pl.semaphore_wait(barrier, n_seq - 1 + n_dp - 1)

    def columns(ref, which):
        return ref.at[:, pl.ds(pl.multiple_of(which * lanes, lanes), lanes)]

    def exchange(i, source, target):
        @pl.loop(1, n_seq)
        def _(hop):
            to = lax.rem(seq + hop, n_seq)
            pltpu.make_async_remote_copy(
                src_ref=source(to),
                dst_ref=target,
                send_sem=send_sem.at[i],
                recv_sem=recv_sem.at[i],
                device_id=(dp, to),
                device_id_type=MESH,
            ).start()

        pltpu.make_async_copy(source(seq), target, recv_sem.at[i]).start()

    def arrived(i, ref):
        pltpu.make_async_copy(ref, ref, recv_sem.at[i]).wait()

    def left(i, ref):
        part = ref.at[pl.ds(0, ref.shape[0] - ref.shape[0] // n_seq)]
        pltpu.make_async_copy(part, part, send_sem.at[i]).wait()

    exchange(0, lambda to: owners_in, own_got.at[seq])
    exchange(1, lambda to: columns(conv, to), conv_got.at[seq])
    exchange(2, lambda to: columns(taps, to), taps_got.at[seq])

    loads[0].wait()
    loads[1].wait()

    @pl.loop(0, rows // tile)
    def _(i):
        at = pl.ds(pl.multiple_of(i * tile, tile), tile)
        mixed_v[at, :] = (up_v[at, :].astype(F32) * gate_v[at, :].astype(F32)).astype(BF16)

    exchange(3, lambda to: columns(mixed_v, to), mixed_got.at[seq])

    def transform(got, into, lane, where):
        @pl.loop(0, rows // tile)
        def _(i):
            at = pl.ds(pl.multiple_of(i * tile, tile), tile)
            low = pl.ds(pl.multiple_of(rows + i * tile, tile), tile)
            found = spectrum_of([got[where(q), at, :].astype(F32) for q in range(n_seq)])
            for k in range(n_seq):
                into[k, at, lane : lane + lanes] = found[k][0].astype(BF16)
                into[k, low, lane : lane + lanes] = found[k][1].astype(BF16)

    def invert(lane, put):
        @pl.loop(0, rows // tile)
        def _(i):
            at = pl.ds(pl.multiple_of(i * tile, tile), tile)
            low = pl.ds(pl.multiple_of(rows + i * tile, tile), tile)
            found = values_of(
                [
                    (turned[k, at, lane : lane + lanes], turned[k, low, lane : lane + lanes])
                    for k in range(n_seq)
                ]
            )
            for q in range(n_seq):
                put(q, at, i, found[q].astype(BF16))

    arrived(0, own_got)
    owner_ids = lax.broadcasted_iota(I32, (n_seq, rows), 0)
    wide = lax.broadcasted_iota(I32, (n_seq, n_seq * slot), 1)
    wide_block, wide_slot = wide // slot, wide % slot
    above = lax.broadcasted_iota(I32, (rows, rows), 0)
    beside = lax.broadcasted_iota(I32, (rows, rows), 1)
    earlier = jnp.where(above < beside, 1.0, 0.0).astype(BF16)

    def place(p, carry):
        so_far, first = carry
        hits = jnp.where(own_got[p, 0:1, :] == owner_ids, 1.0, 0.0)
        count = jnp.sum(hits, axis=1, keepdims=True).astype(I32)
        mine = jnp.logical_and(wide_block == p, wide_slot < count)
        return so_far + count, jnp.where(mine, so_far + wide_slot, first)

    _, first = lax.fori_loop(
        0,
        n_seq,
        place,
        (jnp.zeros((n_seq, 1), I32), jnp.full((n_seq, n_seq * slot), -1, I32)),
    )
    starts[...] = first

    arrived(1, conv_got)
    transform(conv_got, pair_a, 0, lambda q: place_of[q])
    arrived(2, taps_got)
    transform(taps_got, pair_a, lanes, lambda q: q)
    loads[2].wait()
    loads[3].wait()

    @pl.loop(0, n_seq)
    def _(k):
        both = jnp.dot(table[k], pair_a[k], preferred_element_type=F32)
        specs[k] = both
        xr, xi = both[:rows, :lanes], both[rows:, :lanes]
        tr, ti = both[:rows, lanes:], both[rows:, lanes:]
        made = jnp.concatenate([xr * tr - xi * ti, xr * ti + xi * tr], axis=0)
        turned[k, :, :lanes] = jnp.dot(
            back_table[k], made.astype(BF16), preferred_element_type=F32
        )

    def put_signal(q, at, i, found):
        sig_time[q, at, :] = found

    invert(0, put_signal)

    @pl.loop(0, n_seq)
    def _(p):
        sig_send[p] = sig_time[order[p]]

    exchange(4, lambda to: sig_send.at[to], columns(sig_out, seq))

    arrived(3, mixed_got)
    transform(mixed_got, mixed_a, 0, lambda q: place_of[q])

    @pl.loop(0, n_seq)
    def _(k):
        mixed = jnp.dot(table[k], mixed_a[k], preferred_element_type=F32)
        mr, mi = mixed[:rows], mixed[rows:]
        xr, xi = specs[k, :rows, :lanes], specs[k, rows:, :lanes]
        tr, ti = specs[k, :rows, lanes:], specs[k, rows:, lanes:]
        made = jnp.concatenate(
            [
                jnp.concatenate([tr * mr + ti * mi, xr * mr + xi * mi], axis=1),
                jnp.concatenate([tr * mi - ti * mr, xr * mi - xi * mr], axis=1),
            ],
            axis=0,
        )
        turned[k] = jnp.dot(back_table[k], made.astype(BF16), preferred_element_type=F32)

    def put_back(q, at, i, found):
        back_time[q, at, :] = found

    invert(0, put_back)

    def pack(p):
        owner = own_got[p, 0:1, :]
        hits = jnp.where(owner == owner_ids, 1.0, 0.0)
        before = jnp.dot(hits.astype(BF16), earlier, preferred_element_type=F32)
        rank = jnp.sum(hits * before, axis=0, keepdims=True).astype(I32)
        place_ids = lax.broadcasted_iota(I32, (n_seq * slot, rows), 0)
        chosen = jnp.where(owner * slot + rank == place_ids, 1.0, 0.0).astype(BF16)
        found = jnp.dot(chosen, back_time[order[p]], preferred_element_type=F32)
        at = pl.ds(pl.multiple_of(p * slot, slot), slot)
        packed[:, at, :] = found.reshape(n_seq, slot, lanes)

    pl.loop(0, n_seq)(pack)

    @pl.loop(0, n_seq)
    def _(o):
        row_ids = lax.broadcasted_iota(I32, (n_seq * slot, n_seq * slot), 0)
        chosen = jnp.where(starts[pl.ds(o, 1), :] == row_ids, 1.0, 0.0).astype(BF16)
        found = jnp.dot(chosen, packed[o].astype(BF16), preferred_element_type=F32)
        rows_send[o] = found.astype(BF16)

    exchange(5, lambda to: rows_send.at[to], columns(rows_out, seq))

    per = n_seq // n_dp

    def put_filter(q, at, i, found):
        down = pl.ds(pl.multiple_of((q % per) * rows + i * tile, tile), tile)
        filt_send[q // per, down, :] = found

    invert(lanes, put_filter)

    @pl.loop(1, n_dp)
    def _(hop):
        to = lax.rem(dp + hop, n_dp)
        pltpu.make_async_remote_copy(
            src_ref=filt_send.at[to],
            dst_ref=parts_out.at[dp],
            send_sem=send_sem.at[6],
            recv_sem=recv_sem.at[6],
            device_id=(to, seq),
            device_id_type=MESH,
        ).start()

    pltpu.make_async_copy(filt_send.at[dp], parts_out.at[dp], recv_sem.at[6]).start()

    left(0, own_got)
    left(1, conv_got)
    left(2, taps_got)
    left(3, mixed_got)
    left(4, sig_send)
    left(5, rows_send)
    others = filt_send.at[pl.ds(0, n_dp - 1)]
    pltpu.make_async_copy(others, others, send_sem.at[6]).wait()
    arrived(4, sig_out)
    arrived(6, parts_out)
    arrived(5, rows_out)


def per_device(gate_input, conv_input, grad_output, filter_taps, block_order, owner_rows):
    gate_rows, conv_rows, upstream = gate_input[0], conv_input[0], grad_output[0]
    rows, channels = gate_rows.shape
    n_dp, n_seq = lax.axis_size("dp"), lax.axis_size("seq")
    lanes = channels // n_seq
    cap = 2 * rows
    slot = cap // n_seq
    ids = jnp.arange(n_seq, dtype=I32)
    place_of = jnp.sum(jnp.where(block_order[None, :] == ids[:, None], ids[None, :], 0), axis=1)
    table, back_table = tables(n_seq, rows)
    anywhere, scalars = pl.BlockSpec(memory_space=pl.ANY), pl.BlockSpec(memory_space=pltpu.SMEM)
    full = (n_seq, rows, lanes)
    scratch = (
        [pltpu.VMEM((rows, channels), BF16)] * 3
        + [pltpu.VMEM((n_seq, 8, rows), I32)]
        + [pltpu.VMEM(full, BF16)] * 3
        + [pltpu.VMEM((n_seq, 2 * rows, 2 * rows), BF16)] * 2
        + [
            pltpu.VMEM((n_seq, 2 * rows, 2 * lanes), BF16),
            pltpu.VMEM((n_seq, 2 * rows, lanes), BF16),
            pltpu.VMEM((n_seq, 2 * rows, 2 * lanes), F32),
            pltpu.VMEM((n_seq, 2 * rows, 2 * lanes), F32),
        ]
        + [pltpu.VMEM(full, BF16)] * 3
        + [
            pltpu.VMEM((n_seq, n_seq * slot), I32),
            pltpu.VMEM((n_seq, n_seq * slot, lanes), F32),
            pltpu.VMEM((n_seq, cap, lanes), BF16),
            pltpu.VMEM((n_dp, n_seq * rows // n_dp, lanes), BF16),
            pltpu.SemaphoreType.DMA((7,)),
            pltpu.SemaphoreType.DMA((7,)),
            pltpu.SemaphoreType.DMA((4,)),
        ]
    )
    signal, returned, parts = pl.pallas_call(
        functools.partial(kernel, n_dp, n_seq),
        out_shape=(
            jax.ShapeDtypeStruct((rows, channels), BF16),
            jax.ShapeDtypeStruct((cap, channels), BF16),
            jax.ShapeDtypeStruct((n_dp, n_seq * rows // n_dp, lanes), BF16),
        ),
        in_specs=[scalars, scalars] + [anywhere] * 7,
        out_specs=(anywhere,) * 3,
        scratch_shapes=scratch,
        compiler_params=pltpu.CompilerParams(
            collective_id=0, has_side_effects=True, vmem_limit_bytes=VMEM_BYTES
        ),
        name="conv_backward",
    )(
        block_order,
        place_of,
        jnp.broadcast_to(owner_rows, (8, rows)),
        gate_rows,
        conv_rows,
        upstream,
        filter_taps,
        jnp.asarray(table),
        jnp.asarray(back_table),
    )
    grad_gate = (upstream.astype(F32) * signal.astype(F32)).astype(BF16)
    grad_filter = jnp.sum(parts.astype(F32), axis=0)
    return grad_gate[None], returned[None], grad_filter


def solution(mesh):
    placed = (
        P("dp", "seq", None),
        P("dp", "seq", None),
        P("dp", "seq", None),
        P("seq", None),
        P(),
        P("dp", "seq"),
    )
    return jax.shard_map(
        per_device,
        mesh=mesh,
        in_specs=placed,
        out_specs=(P("dp", "seq", None), P("dp", "seq", None), P("dp", "seq")),
        check_vma=False,
    )
```

profile of v0, /device:TPU:9, one launch (start us, length us, event | category | flops | bytes accessed | tf_op | source)
XLA Modules:
  0.0 134.1 jit_solution(10235853095184361995)
XLA Ops:
  0.6 1.3 select_reduce_fusion.place_of
  1.9 1.2 broadcast_in_dim.31.owners_in
  3.2 0.0 copy-start
  3.2 126.2 %conv_backward.1 = (bf16[128,4096]{1,0:T(8,128)(2,1)}, bf16[256,4096]{1,0:T(8,128)(2,1)}, bf16[8,512,128]{2,1,0:T(8,128)(2,1)}) custom-call(s32[32]{0:T(128)} %order.1, s32[32]{0:T(128)} %select_reduce_fusion.place_of, s32[8,128]{1,0:T(8,128)} %broadcast_in_dim.31.owners_in, bf16[128,4096]{1,0:T(8,128)(2,1)} %bitcast.10, bf16[128,4096]{1,0:T(8,128)(2,1)} %bitcast.11, ...), custom_call_target="tpu_custom_call" | custom-call | tf_op jit(solution)/shard_map/conv_backward/pallas_call | solution.py:363
  129.3 0.0 copy-start.2
  129.3 0.0 copy-done
  129.4 0.0 copy-start.1
  129.4 2.6 %fusion = bf16[1,128,4096]{2,1,0:T(8,128)(2,1)} fusion(bf16[128,4096]{1,0:T(8,128)(2,1)} %get-tuple-element.6, bf16[1,128,4096]{2,1,0:T(8,128)(2,1)S(1)} %copy-done), kind=kLoop, calls=%fused_computation.2 | loop fusion | flops 2097152 | bytes 3145728 | tf_op jit(solution)/shard_map/broadcast_in_dim | solution.py:390
  132.0 0.0 copy-done.2
  132.0 0.8 convert_reduce_fusion
  132.8 0.0 copy-done.1
  132.8 1.3 copy.12
Async XLA Ops:
  3.2 126.2 %copy-start = (bf16[1,128,4096]{2,1,0:T(8,128)(2,1)S(1)}, bf16[1,128,4096]{2,1,0:T(8,128)(2,1)}, u32[]{:S(2)}) copy-start(bf16[1,128,4096]{2,1,0:T(8,128)(2,1)} %param.10) | copy-start | bytes 3145732
  129.3 2.6 %copy-start.2 = (bf16[8,512,128]{2,1,0:T(8,128)(2,1)S(1)}, bf16[8,512,128]{2,1,0:T(8,128)(2,1)}, u32[]{:S(2)}) copy-start(bf16[8,512,128]{2,1,0:T(8,128)(2,1)} %get-tuple-element.8) | copy-start | bytes 3145732
  129.4 3.5 %copy-start.1 = (bf16[256,4096]{1,0:T(8,128)(2,1)S(1)}, bf16[256,4096]{1,0:T(8,128)(2,1)}, u32[]{:S(2)}) copy-start(bf16[256,4096]{1,0:T(8,128)(2,1)} %get-tuple-element.7) | copy-start | bytes 6291460
where the time goes:
time: 134 us
  Pallas kernels  126 us (94%)
  other arithmetic  4.73 us (4%)
  local copies, waits for them, and re-layouts  2.58 us (2%)
    pallas_call x1, Pallas kernels, per_device(): pl.pallas_call(functools.partial(kernel, n_dp, n_seq), out_shape=(jax.Sha...  126 us

commit v1 on v0

--- a/solution.py
+++ b/solution.py
@@ -67,7 +67,6 @@
     n_dp,
     n_seq,
     order,
-    place_of,
     owners_in,
     gate,
     conv,
@@ -75,12 +74,14 @@
     taps,
     table_in,
     back_in,
-    sig_out,
+    gate_out,
     rows_out,
-    parts_out,
+    filter_out,
+    place_of,
     gate_v,
     up_v,
     mixed_v,
+    sig_got,
     own_got,
     conv_got,
     taps_got,
@@ -88,16 +89,19 @@
     table,
     back_table,
     pair_a,
-    mixed_a,
     specs,
     turned,
     sig_time,
     sig_send,
     back_time,
     starts,
+    slot_of,
+    row_of,
     packed,
     rows_send,
     filt_send,
+    parts_got,
+    filt_sum,
     send_sem,
     recv_sem,
     local_sem,
@@ -107,6 +111,7 @@
     lanes = conv_got.shape[2]
     tile = 16
     slot = rows_send.shape[1] // n_seq
+    side = math.isqrt(n_seq // 2)
 
     loads = [
         pltpu.make_async_copy(a, b, local_sem.at[i])
@@ -134,10 +139,19 @@
     def columns(ref, which):
         return ref.at[:, pl.ds(pl.multiple_of(which * lanes, lanes), lanes)]
 
+    core, place_x, place_y = seq % 2, seq // 2 % side, seq // (2 * side)
+    odd, sign = (place_x + place_y) % 2, 1 - 2 * core
+
+    def partner(hop):
+        u, v = hop // 2 % side, hop // (2 * side)
+        dx, dy = odd * v + (1 - odd) * u, odd * u + (1 - odd) * v
+        y, x = (place_y + side + sign * dy) % side, (place_x + side + sign * dx) % side
+        return (y * side + x) * 2 + (core + hop) % 2
+
     def exchange(i, source, target):
         @pl.loop(1, n_seq)
         def _(hop):
-            to = lax.rem(seq + hop, n_seq)
+            to = partner(hop)
             pltpu.make_async_remote_copy(
                 src_ref=source(to),
                 dst_ref=target,
@@ -156,7 +170,7 @@
         part = ref.at[pl.ds(0, ref.shape[0] - ref.shape[0] // n_seq)]
         pltpu.make_async_copy(part, part, send_sem.at[i]).wait()
 
-    exchange(0, lambda to: owners_in, own_got.at[seq])
+    exchange(0, lambda to: owners_in, own_got.at[pl.ds(seq, 1)])
     exchange(1, lambda to: columns(conv, to), conv_got.at[seq])
     exchange(2, lambda to: columns(taps, to), taps_got.at[seq])
 
@@ -194,6 +208,13 @@
             for q in range(n_seq):
                 put(q, at, i, found[q].astype(BF16))
 
+    @pl.loop(0, n_seq)
+    def _(q):
+        found = 0
+        for p in range(n_seq):
+            found = jnp.where(order[p] == q, p, found)
+        place_of[q] = found
+
     arrived(0, own_got)
     owner_ids = lax.broadcasted_iota(I32, (n_seq, rows), 0)
     wide = lax.broadcasted_iota(I32, (n_seq, n_seq * slot), 1)
@@ -204,7 +225,8 @@
 
     def place(p, carry):
         so_far, first = carry
-        hits = jnp.where(own_got[p, 0:1, :] == owner_ids, 1.0, 0.0)
+        owner = own_got[pl.ds(p, 1), :]
+        hits = jnp.where(owner == owner_ids, 1.0, 0.0)
         count = jnp.sum(hits, axis=1, keepdims=True).astype(I32)
         mine = jnp.logical_and(wide_block == p, wide_slot < count)
         return so_far + count, jnp.where(mine, so_far + wide_slot, first)
@@ -217,6 +239,20 @@
     )
     starts[...] = first
 
+    @pl.loop(0, n_seq, unroll=4)
+    def _(p):
+        owner = own_got[pl.ds(p, 1), :]
+        hits = jnp.where(owner == owner_ids, 1.0, 0.0)
+        before = jnp.dot(hits.astype(BF16), earlier, preferred_element_type=F32)
+        rank = jnp.sum(hits * before, axis=0, keepdims=True).astype(I32)
+        place_ids = lax.broadcasted_iota(I32, (n_seq * slot, rows), 0)
+        slot_of[p] = jnp.where(owner * slot + rank == place_ids, 1.0, 0.0).astype(BF16)
+
+    @pl.loop(0, n_seq, unroll=4)
+    def _(o):
+        row_ids = lax.broadcasted_iota(I32, (n_seq * slot, n_seq * slot), 0)
+        row_of[o] = jnp.where(starts[pl.ds(o, 1), :] == row_ids, 1.0, 0.0).astype(BF16)
+
     arrived(1, conv_got)
     transform(conv_got, pair_a, 0, lambda q: place_of[q])
     arrived(2, taps_got)
@@ -224,7 +260,7 @@
     loads[2].wait()
     loads[3].wait()
 
-    @pl.loop(0, n_seq)
+    @pl.loop(0, n_seq, unroll=4)
     def _(k):
         both = jnp.dot(table[k], pair_a[k], preferred_element_type=F32)
         specs[k] = both
@@ -244,14 +280,14 @@
     def _(p):
         sig_send[p] = sig_time[order[p]]
 
-    exchange(4, lambda to: sig_send.at[to], columns(sig_out, seq))
+    exchange(4, lambda to: sig_send.at[to], columns(sig_got, seq))
 
     arrived(3, mixed_got)
-    transform(mixed_got, mixed_a, 0, lambda q: place_of[q])
-
-    @pl.loop(0, n_seq)
+    transform(mixed_got, pair_a, 0, lambda q: place_of[q])
+
+    @pl.loop(0, n_seq, unroll=4)
     def _(k):
-        mixed = jnp.dot(table[k], mixed_a[k], preferred_element_type=F32)
+        mixed = jnp.dot(table[k], pair_a[k, :, :lanes], preferred_element_type=F32)
         mr, mi = mixed[:rows], mixed[rows:]
         xr, xi = specs[k, :rows, :lanes], specs[k, rows:, :lanes]
         tr, ti = specs[k, :rows, lanes:], specs[k, rows:, lanes:]
@@ -269,24 +305,15 @@
 
     invert(0, put_back)
 
-    def pack(p):
-        owner = own_got[p, 0:1, :]
-        hits = jnp.where(owner == owner_ids, 1.0, 0.0)
-        before = jnp.dot(hits.astype(BF16), earlier, preferred_element_type=F32)
-        rank = jnp.sum(hits * before, axis=0, keepdims=True).astype(I32)
-        place_ids = lax.broadcasted_iota(I32, (n_seq * slot, rows), 0)
-        chosen = jnp.where(owner * slot + rank == place_ids, 1.0, 0.0).astype(BF16)
-        found = jnp.dot(chosen, back_time[order[p]], preferred_element_type=F32)
+    @pl.loop(0, n_seq, unroll=4)
+    def _(p):
+        found = jnp.dot(slot_of[p], back_time[order[p]], preferred_element_type=F32)
         at = pl.ds(pl.multiple_of(p * slot, slot), slot)
         packed[:, at, :] = found.reshape(n_seq, slot, lanes)
 
-    pl.loop(0, n_seq)(pack)
-
-    @pl.loop(0, n_seq)
+    @pl.loop(0, n_seq, unroll=4)
     def _(o):
-        row_ids = lax.broadcasted_iota(I32, (n_seq * slot, n_seq * slot), 0)
-        chosen = jnp.where(starts[pl.ds(o, 1), :] == row_ids, 1.0, 0.0).astype(BF16)
-        found = jnp.dot(chosen, packed[o].astype(BF16), preferred_element_type=F32)
+        found = jnp.dot(row_of[o], packed[o].astype(BF16), preferred_element_type=F32)
         rows_send[o] = found.astype(BF16)
 
     exchange(5, lambda to: rows_send.at[to], columns(rows_out, seq))
@@ -304,15 +331,36 @@
         to = lax.rem(dp + hop, n_dp)
         pltpu.make_async_remote_copy(
             src_ref=filt_send.at[to],
-            dst_ref=parts_out.at[dp],
+            dst_ref=parts_got.at[dp],
             send_sem=send_sem.at[6],
             recv_sem=recv_sem.at[6],
             device_id=(to, seq),
             device_id_type=MESH,
         ).start()
 
-    pltpu.make_async_copy(filt_send.at[dp], parts_out.at[dp], recv_sem.at[6]).start()
-
+    pltpu.make_async_copy(filt_send.at[dp], parts_got.at[dp], recv_sem.at[6]).start()
+
+    arrived(4, sig_got)
+
+    @pl.loop(0, rows // tile)
+    def _(i):
+        at = pl.ds(pl.multiple_of(i * tile, tile), tile)
+        gate_v[at, :] = (up_v[at, :].astype(F32) * sig_got[at, :].astype(F32)).astype(BF16)
+
+    gate_copy = pltpu.make_async_copy(gate_v, gate_out, local_sem.at[0])
+    gate_copy.start()
+    arrived(6, parts_got)
+
+    @pl.loop(0, per * rows // tile)
+    def _(i):
+        at = pl.ds(pl.multiple_of(i * tile, tile), tile)
+        total = parts_got[0, at, :].astype(F32)
+        for z in range(1, n_dp):
+            total = total + parts_got[z, at, :].astype(F32)
+        filt_sum[at, :] = total
+
+    filter_copy = pltpu.make_async_copy(filt_sum, filter_out, local_sem.at[1])
+    filter_copy.start()
     left(0, own_got)
     left(1, conv_got)
     left(2, taps_got)
@@ -321,8 +369,8 @@
     left(5, rows_send)
     others = filt_send.at[pl.ds(0, n_dp - 1)]
     pltpu.make_async_copy(others, others, send_sem.at[6]).wait()
-    arrived(4, sig_out)
-    arrived(6, parts_out)
+    gate_copy.wait()
+    filter_copy.wait()
     arrived(5, rows_out)
 
 
@@ -333,41 +381,41 @@
     lanes = channels // n_seq
     cap = 2 * rows
     slot = cap // n_seq
-    ids = jnp.arange(n_seq, dtype=I32)
-    place_of = jnp.sum(jnp.where(block_order[None, :] == ids[:, None], ids[None, :], 0), axis=1)
     table, back_table = tables(n_seq, rows)
     anywhere, scalars = pl.BlockSpec(memory_space=pl.ANY), pl.BlockSpec(memory_space=pltpu.SMEM)
     full = (n_seq, rows, lanes)
-    scratch = (
-        [pltpu.VMEM((rows, channels), BF16)] * 3
-        + [pltpu.VMEM((n_seq, 8, rows), I32)]
-        + [pltpu.VMEM(full, BF16)] * 3
-        + [pltpu.VMEM((n_seq, 2 * rows, 2 * rows), BF16)] * 2
-        + [
-            pltpu.VMEM((n_seq, 2 * rows, 2 * lanes), BF16),
-            pltpu.VMEM((n_seq, 2 * rows, lanes), BF16),
-            pltpu.VMEM((n_seq, 2 * rows, 2 * lanes), F32),
-            pltpu.VMEM((n_seq, 2 * rows, 2 * lanes), F32),
-        ]
-        + [pltpu.VMEM(full, BF16)] * 3
-        + [
-            pltpu.VMEM((n_seq, n_seq * slot), I32),
-            pltpu.VMEM((n_seq, n_seq * slot, lanes), F32),
-            pltpu.VMEM((n_seq, cap, lanes), BF16),
-            pltpu.VMEM((n_dp, n_seq * rows // n_dp, lanes), BF16),
-            pltpu.SemaphoreType.DMA((7,)),
-            pltpu.SemaphoreType.DMA((7,)),
-            pltpu.SemaphoreType.DMA((4,)),
-        ]
-    )
-    signal, returned, parts = pl.pallas_call(
+    square = (n_seq, 2 * rows, 2 * lanes)
+    parts = (n_dp, n_seq * rows // n_dp, lanes)
+    scratch = [
+        pltpu.SMEM((n_seq,), I32),
+        *[pltpu.VMEM((rows, channels), BF16)] * 4,
+        pltpu.VMEM((n_seq, rows), I32),
+        *[pltpu.VMEM(full, BF16)] * 3,
+        *[pltpu.VMEM((n_seq, 2 * rows, 2 * rows), BF16)] * 2,
+        pltpu.VMEM(square, BF16),
+        pltpu.VMEM(square, F32),
+        pltpu.VMEM(square, F32),
+        *[pltpu.VMEM(full, BF16)] * 3,
+        pltpu.VMEM((n_seq, cap), I32),
+        pltpu.VMEM((n_seq, cap, rows), BF16),
+        pltpu.VMEM((n_seq, cap, cap), BF16),
+        pltpu.VMEM((n_seq, cap, lanes), F32),
+        pltpu.VMEM((n_seq, cap, lanes), BF16),
+        pltpu.VMEM(parts, BF16),
+        pltpu.VMEM(parts, BF16),
+        pltpu.VMEM(parts[1:], F32),
+        pltpu.SemaphoreType.DMA((7,)),
+        pltpu.SemaphoreType.DMA((7,)),
+        pltpu.SemaphoreType.DMA((4,)),
+    ]
+    grad_gate, returned, grad_filter = pl.pallas_call(
         functools.partial(kernel, n_dp, n_seq),
         out_shape=(
             jax.ShapeDtypeStruct((rows, channels), BF16),
             jax.ShapeDtypeStruct((cap, channels), BF16),
-            jax.ShapeDtypeStruct((n_dp, n_seq * rows // n_dp, lanes), BF16),
+            jax.ShapeDtypeStruct(parts[1:], F32),
         ),
-        in_specs=[scalars, scalars] + [anywhere] * 7,
+        in_specs=[scalars] + [anywhere] * 7,
         out_specs=(anywhere,) * 3,
         scratch_shapes=scratch,
         compiler_params=pltpu.CompilerParams(
@@ -376,8 +424,7 @@
         name="conv_backward",
     )(
         block_order,
-        place_of,
-        jnp.broadcast_to(owner_rows, (8, rows)),
+        owner_rows,
         gate_rows,
         conv_rows,
         upstream,
@@ -385,8 +432,6 @@
         jnp.asarray(table),
         jnp.asarray(back_table),
     )
-    grad_gate = (upstream.astype(F32) * signal.astype(F32)).astype(BF16)
-    grad_filter = jnp.sum(parts.astype(F32), axis=0)
     return grad_gate[None], returned[None], grad_filter
 
 

time: 134 us -> 99.5 us (0.74)
  Pallas kernels: 126 us -> 92.1 us
  other arithmetic: 4.73 us -> 0 us
  local copies, waits for them, and re-layouts: 2.58 us -> 6.16 us
    pallas_call x1, Pallas kernels: 126 us -> 92.1 us  [per_device(): pl.pallas_call(functools.partial(kernel, n_dp, n_seq), out_shape=(jax.Sha...]
    unnamed x7 -> x5, local copies, waits for them, and re-layouts: 1.33 us -> 6.16 us
    broadcast_in_dim x1 -> x0, other arithmetic: 2.6 us -> none  [per_device(): return (grad_gate[None], returned[None], grad_filter)]
    reduce_sum x2 -> x0, other arithmetic: 2.13 us -> none  [the longest x1 1.28 us: per_device(): jnp.sum(jnp.where(block_order[None, :] == ids[:, None], ids[None, :], 0),...]
where the time goes in v1:
time: 99.5 us; the launch traced here: 98.9 us
  Pallas kernels  92.1 us (93%)
  local copies, waits for them, and re-layouts  6.16 us (6%)
    pallas_call x1, Pallas kernels, per_device(): pl.pallas_call(functools.partial(kernel, n_dp, n_seq), out_shape=(jax.Sha...  92.1 us
    unnamed x5, local copies, waits for them, and re-layouts  6.16 us

profile of v1, /device:TPU:9, one launch (start us, length us, event | category | flops | bytes accessed | tf_op | source)
XLA Modules:
  0.0 98.9 jit_solution(6824708323667983967)
XLA Ops:
  0.6 92.1 %conv_backward.1 = (bf16[128,4096]{1,0:T(8,128)(2,1)}, bf16[256,4096]{1,0:T(8,128)(2,1)}, f32[512,128]{1,0:T(8,128)}) custom-call(s32[32]{0:T(128)} %order.1, s32[1,128]{1,0:T(1,128)} %owners_in.1, bf16[128,4096]{1,0:T(8,128)(2,1)} %bitcast.6, bf16[128,4096]{1,0:T(8,128)(2,1)} %bitcast.7, bf16[128,4096]{1,0:T(8,128)(2,1)} %bitcast.8, ...), custom_call_target="tpu_custom_call" | custom-call | tf_op jit(solution)/shard_map/conv_backward/pallas_call | solution.py:411
  92.7 0.0 copy-start
  92.8 2.3 %copy.14 = bf16[1,128,4096]{2,1,0:T(8,128)(2,1)} copy(bf16[1,128,4096]{2,1,0:T(8,128)(2,1)} %bitcast.9) | data formatting | bytes 2097152
  95.1 3.1 %copy.15 = bf16[1,256,4096]{2,1,0:T(8,128)(2,1)} copy(bf16[1,256,4096]{2,1,0:T(8,128)(2,1)} %bitcast.5) | data formatting | bytes 4194304
  98.2 0.0 copy-done
  98.2 0.7 copy.16
Async XLA Ops:
  92.7 5.5 %copy-start = (f32[512,128]{1,0:T(8,128)S(1)}, f32[512,128]{1,0:T(8,128)}, u32[]{:S(2)}) copy-start(f32[512,128]{1,0:T(8,128)} %get-tuple-element.14) | copy-start | bytes 786436

commit v2 on v1

--- a/solution.py
+++ b/solution.py
@@ -11,7 +11,7 @@
 
 F32, BF16, I32 = jnp.float32, jnp.bfloat16, jnp.int32
 MESH = pl.DeviceIdType.MESH
-VMEM_BYTES = 60 * 2**20
+VMEM_BYTES = 58 * 2**20
 
 
 def spectrum_of(values):
@@ -101,10 +101,11 @@
     rows_send,
     filt_send,
     parts_got,
-    filt_sum,
     send_sem,
     recv_sem,
     local_sem,
+    ring_send,
+    ring_recv,
 ):
     dp, seq = lax.axis_index("dp"), lax.axis_index("seq")
     rows = gate_v.shape[0]
@@ -116,7 +117,12 @@
     loads = [
         pltpu.make_async_copy(a, b, local_sem.at[i])
         for i, (a, b) in enumerate(
-            ((gate, gate_v), (upstream, up_v), (table_in, table), (back_in, back_table))
+            (
+                (gate, gate_v),
+                (upstream, up_v),
+                (table_in, table),
+                (back_in, back_table),
+            )
         )
     ]
     for load in loads:
@@ -171,9 +177,9 @@
         pltpu.make_async_copy(part, part, send_sem.at[i]).wait()
 
     exchange(0, lambda to: owners_in, own_got.at[pl.ds(seq, 1)])
+    share = taps.at[pl.ds(pl.multiple_of(dp * tile, tile), tile)]
+    exchange(2, lambda to: columns(share, to), taps_got.at[dp, seq])
     exchange(1, lambda to: columns(conv, to), conv_got.at[seq])
-    exchange(2, lambda to: columns(taps, to), taps_got.at[seq])
-
     loads[0].wait()
     loads[1].wait()
 
@@ -184,12 +190,43 @@
 
     exchange(3, lambda to: columns(mixed_v, to), mixed_got.at[seq])
 
-    def transform(got, into, lane, where):
+    def ring(step):
+        halves = step == n_dp // 2 - 1
+        parts = (pl.ds(0, n_seq // 2), pl.ds(n_seq // 2, n_seq // 2)) if halves else (pl.ds(0, n_seq),) * 2
+        copies = []
+        for way, turn in enumerate((1, -1)):
+            held = taps_got.at[lax.rem(dp - turn * step + n_dp, n_dp), parts[way]]
+            copies.append(
+                pltpu.make_async_remote_copy(
+                    src_ref=held,
+                    dst_ref=held,
+                    send_sem=ring_send.at[2 * step + way],
+                    recv_sem=ring_recv.at[2 * step + way],
+                    device_id=(lax.rem(dp + turn + n_dp, n_dp), seq),
+                    device_id_type=MESH,
+                )
+            )
+        return copies
+
+    rings = [ring(step) for step in range(n_dp // 2)]
+
+    def send_on(step):
+        for copy in rings[step]:
+            copy.start()
+
+    def met(step):
+        for copy in rings[step]:
+            copy.wait_recv()
+
+    arrived(2, taps_got.at[dp])
+    send_on(0)
+
+    def transform(load, into, lane):
         @pl.loop(0, rows // tile)
         def _(i):
             at = pl.ds(pl.multiple_of(i * tile, tile), tile)
             low = pl.ds(pl.multiple_of(rows + i * tile, tile), tile)
-            found = spectrum_of([got[where(q), at, :].astype(F32) for q in range(n_seq)])
+            found = spectrum_of([load(q, at, i).astype(F32) for q in range(n_seq)])
             for k in range(n_seq):
                 into[k, at, lane : lane + lanes] = found[k][0].astype(BF16)
                 into[k, low, lane : lane + lanes] = found[k][1].astype(BF16)
@@ -238,6 +275,8 @@
         (jnp.zeros((n_seq, 1), I32), jnp.full((n_seq, n_seq * slot), -1, I32)),
     )
     starts[...] = first
+    met(0)
+    send_on(1)
 
     @pl.loop(0, n_seq, unroll=4)
     def _(p):
@@ -248,15 +287,20 @@
         place_ids = lax.broadcasted_iota(I32, (n_seq * slot, rows), 0)
         slot_of[p] = jnp.where(owner * slot + rank == place_ids, 1.0, 0.0).astype(BF16)
 
+    met(1)
+    send_on(2)
+
     @pl.loop(0, n_seq, unroll=4)
     def _(o):
         row_ids = lax.broadcasted_iota(I32, (n_seq * slot, n_seq * slot), 0)
         row_of[o] = jnp.where(starts[pl.ds(o, 1), :] == row_ids, 1.0, 0.0).astype(BF16)
 
+    met(2)
+    send_on(3)
     arrived(1, conv_got)
-    transform(conv_got, pair_a, 0, lambda q: place_of[q])
-    arrived(2, taps_got)
-    transform(taps_got, pair_a, lanes, lambda q: q)
+    transform(lambda q, at, i: conv_got[place_of[q], at, :], pair_a, 0)
+    met(3)
+    transform(lambda q, at, i: taps_got[i, q], pair_a, lanes)
     loads[2].wait()
     loads[3].wait()
 
@@ -283,7 +327,7 @@
     exchange(4, lambda to: sig_send.at[to], columns(sig_got, seq))
 
     arrived(3, mixed_got)
-    transform(mixed_got, pair_a, 0, lambda q: place_of[q])
+    transform(lambda q, at, i: mixed_got[place_of[q], at, :], pair_a, 0)
 
     @pl.loop(0, n_seq, unroll=4)
     def _(k):
@@ -345,10 +389,8 @@
     @pl.loop(0, rows // tile)
     def _(i):
         at = pl.ds(pl.multiple_of(i * tile, tile), tile)
-        gate_v[at, :] = (up_v[at, :].astype(F32) * sig_got[at, :].astype(F32)).astype(BF16)
-
-    gate_copy = pltpu.make_async_copy(gate_v, gate_out, local_sem.at[0])
-    gate_copy.start()
+        gate_out[at, :] = (up_v[at, :].astype(F32) * sig_got[at, :].astype(F32)).astype(BF16)
+
     arrived(6, parts_got)
 
     @pl.loop(0, per * rows // tile)
@@ -357,20 +399,19 @@
         total = parts_got[0, at, :].astype(F32)
         for z in range(1, n_dp):
             total = total + parts_got[z, at, :].astype(F32)
-        filt_sum[at, :] = total
-
-    filter_copy = pltpu.make_async_copy(filt_sum, filter_out, local_sem.at[1])
-    filter_copy.start()
+        filter_out[at, :] = total
+
     left(0, own_got)
     left(1, conv_got)
-    left(2, taps_got)
+    left(2, taps_got.at[dp])
+    for copies in rings:
+        for copy in copies:
+            copy.wait_send()
     left(3, mixed_got)
     left(4, sig_send)
     left(5, rows_send)
     others = filt_send.at[pl.ds(0, n_dp - 1)]
     pltpu.make_async_copy(others, others, send_sem.at[6]).wait()
-    gate_copy.wait()
-    filter_copy.wait()
     arrived(5, rows_out)
 
 
@@ -390,7 +431,9 @@
         pltpu.SMEM((n_seq,), I32),
         *[pltpu.VMEM((rows, channels), BF16)] * 4,
         pltpu.VMEM((n_seq, rows), I32),
-        *[pltpu.VMEM(full, BF16)] * 3,
+        pltpu.VMEM(full, BF16),
+        pltpu.VMEM((n_dp, n_seq, rows // n_dp, lanes), BF16),
+        pltpu.VMEM(full, BF16),
         *[pltpu.VMEM((n_seq, 2 * rows, 2 * rows), BF16)] * 2,
         pltpu.VMEM(square, BF16),
         pltpu.VMEM(square, F32),
@@ -403,20 +446,21 @@
         pltpu.VMEM((n_seq, cap, lanes), BF16),
         pltpu.VMEM(parts, BF16),
         pltpu.VMEM(parts, BF16),
-        pltpu.VMEM(parts[1:], F32),
         pltpu.SemaphoreType.DMA((7,)),
         pltpu.SemaphoreType.DMA((7,)),
         pltpu.SemaphoreType.DMA((4,)),
+        pltpu.SemaphoreType.DMA((n_dp,)),
+        pltpu.SemaphoreType.DMA((n_dp,)),
     ]
     grad_gate, returned, grad_filter = pl.pallas_call(
         functools.partial(kernel, n_dp, n_seq),
         out_shape=(
-            jax.ShapeDtypeStruct((rows, channels), BF16),
-            jax.ShapeDtypeStruct((cap, channels), BF16),
-            jax.ShapeDtypeStruct(parts[1:], F32),
+            pltpu.VMEM((rows, channels), BF16),
+            pltpu.VMEM((cap, channels), BF16),
+            pltpu.VMEM(parts[1:], F32),
         ),
         in_specs=[scalars] + [anywhere] * 7,
-        out_specs=(anywhere,) * 3,
+        out_specs=(pl.BlockSpec(memory_space=pltpu.VMEM),) * 3,
         scratch_shapes=scratch,
         compiler_params=pltpu.CompilerParams(
             collective_id=0, has_side_effects=True, vmem_limit_bytes=VMEM_BYTES

time: 99.5 us -> 91.7 us (0.922)
  Pallas kernels: 92.1 us -> 87.5 us
  local copies, waits for them, and re-layouts: 6.16 us -> 2.99 us
    pallas_call x1, Pallas kernels: 92.1 us -> 87.5 us  [per_device(): pl.pallas_call(functools.partial(kernel, n_dp, n_seq), out_shape=(pltpu.V...]
    unnamed x5 -> x3, local copies, waits for them, and re-layouts: 6.16 us -> 2.99 us
where the time goes in v2:
time: 91.7 us; the launch traced here: 91.2 us
  Pallas kernels  87.5 us (95%)
  local copies, waits for them, and re-layouts  2.99 us (3%)
    pallas_call x1, Pallas kernels, per_device(): pl.pallas_call(functools.partial(kernel, n_dp, n_seq), out_shape=(pltpu.V...  87.5 us
    unnamed x3, local copies, waits for them, and re-layouts  2.99 us

profile of v2, /device:TPU:9, one launch (start us, length us, event | category | flops | bytes accessed | tf_op | source)
XLA Modules:
  0.0 91.2 jit_solution(14066311208109165991)
XLA Ops:
  0.6 87.5 %conv_backward.1 = (bf16[128,4096]{1,0:T(8,128)(2,1)S(1)}, bf16[256,4096]{1,0:T(8,128)(2,1)S(1)}, f32[512,128]{1,0:T(8,128)S(1)}) custom-call(s32[32]{0:T(128)} %order.1, s32[1,128]{1,0:T(1,128)} %owners_in.1, bf16[128,4096]{1,0:T(8,128)(2,1)} %bitcast.7, bf16[128,4096]{1,0:T(8,128)(2,1)} %bitcast.8, bf16[128,4096]{1,0:T(8,128)(2,1)} %bitcast.9, ...), custom_call_target="tpu_custom_call" | custom-call | tf_op jit(solution)/shard_map/conv_backward/pallas_call | solution.py:455
  88.2 1.0 %copy.14 = bf16[1,128,4096]{2,1,0:T(8,128)(2,1)} copy(bf16[1,128,4096]{2,1,0:T(8,128)(2,1)S(1)} %bitcast.6) | data formatting | bytes 2097152
  89.1 1.3 %copy.15 = bf16[1,256,4096]{2,1,0:T(8,128)(2,1)} copy(bf16[1,256,4096]{2,1,0:T(8,128)(2,1)S(1)} %bitcast.5) | data formatting | bytes 4194304
  90.5 0.7 copy.16

commit v3 on v2

--- a/solution.py
+++ b/solution.py
@@ -154,18 +154,21 @@
         y, x = (place_y + side + sign * dy) % side, (place_x + side + sign * dx) % side
         return (y * side + x) * 2 + (core + hop) % 2
 
+    def remote(i, source, target, to):
+        return pltpu.make_async_remote_copy(
+            src_ref=source,
+            dst_ref=target,
+            send_sem=send_sem.at[i],
+            recv_sem=recv_sem.at[i],
+            device_id=(dp, to),
+            device_id_type=MESH,
+        )
+
     def exchange(i, source, target):
         @pl.loop(1, n_seq)
         def _(hop):
             to = partner(hop)
-            pltpu.make_async_remote_copy(
-                src_ref=source(to),
-                dst_ref=target,
-                send_sem=send_sem.at[i],
-                recv_sem=recv_sem.at[i],
-                device_id=(dp, to),
-                device_id_type=MESH,
-            ).start()
+            remote(i, source(to), target, to).start()
 
         pltpu.make_async_copy(source(seq), target, recv_sem.at[i]).start()
 
@@ -304,7 +307,7 @@
     loads[2].wait()
     loads[3].wait()
 
-    @pl.loop(0, n_seq, unroll=4)
+    @pl.loop(0, n_seq, unroll=16)
     def _(k):
         both = jnp.dot(table[k], pair_a[k], preferred_element_type=F32)
         specs[k] = both
@@ -329,7 +332,7 @@
     arrived(3, mixed_got)
     transform(lambda q, at, i: mixed_got[place_of[q], at, :], pair_a, 0)
 
-    @pl.loop(0, n_seq, unroll=4)
+    @pl.loop(0, n_seq, unroll=16)
     def _(k):
         mixed = jnp.dot(table[k], pair_a[k, :, :lanes], preferred_element_type=F32)
         mr, mi = mixed[:rows], mixed[rows:]
@@ -349,18 +352,31 @@
 
     invert(0, put_back)
 
-    @pl.loop(0, n_seq, unroll=4)
+    @pl.loop(0, n_seq, unroll=8)
     def _(p):
         found = jnp.dot(slot_of[p], back_time[order[p]], preferred_element_type=F32)
         at = pl.ds(pl.multiple_of(p * slot, slot), slot)
         packed[:, at, :] = found.reshape(n_seq, slot, lanes)
 
-    @pl.loop(0, n_seq, unroll=4)
-    def _(o):
-        found = jnp.dot(row_of[o], packed[o].astype(BF16), preferred_element_type=F32)
-        rows_send[o] = found.astype(BF16)
-
-    exchange(5, lambda to: rows_send.at[to], columns(rows_out, seq))
+    together = 8
+
+    @pl.loop(0, n_seq // together)
+    def _(group):
+        partners = [partner(group * together + step) for step in range(together)]
+        for to in partners:
+            found = jnp.dot(row_of[to], packed[to].astype(BF16), preferred_element_type=F32)
+            rows_send[to] = found.astype(BF16)
+        for step, to in enumerate(partners):
+            copy = remote(5, rows_send.at[to], columns(rows_out, seq), to)
+            if step:
+                copy.start()
+                continue
+            pl.when(group > 0)(copy.start)
+
+            @pl.when(group == 0)
+            def _():
+                own = rows_send.at[seq]
+                pltpu.make_async_copy(own, columns(rows_out, seq), recv_sem.at[5]).start()
 
     per = n_seq // n_dp
 

time: 91.7 us -> 85.7 us (0.935)
  Pallas kernels: 87.5 us -> 81.6 us
    pallas_call x1, Pallas kernels: 87.5 us -> 81.6 us  [per_device(): pl.pallas_call(functools.partial(kernel, n_dp, n_seq), out_shape=(pltpu.V...]
where the time goes in v3:
time: 85.7 us; the launch traced here: 85.3 us
  Pallas kernels  81.6 us (95%)
  local copies, waits for them, and re-layouts  2.99 us (3%)
    pallas_call x1, Pallas kernels, per_device(): pl.pallas_call(functools.partial(kernel, n_dp, n_seq), out_shape=(pltpu.V...  81.6 us
    unnamed x3, local copies, waits for them, and re-layouts  2.99 us

profile of v3, /device:TPU:9, one launch (start us, length us, event | category | flops | bytes accessed | tf_op | source)
XLA Modules:
  0.0 85.3 jit_solution(17625893993051085611)
XLA Ops:
  0.6 81.6 %conv_backward.1 = (bf16[128,4096]{1,0:T(8,128)(2,1)S(1)}, bf16[256,4096]{1,0:T(8,128)(2,1)S(1)}, f32[512,128]{1,0:T(8,128)S(1)}) custom-call(s32[32]{0:T(128)} %order.1, s32[1,128]{1,0:T(1,128)} %owners_in.1, bf16[128,4096]{1,0:T(8,128)(2,1)} %bitcast.7, bf16[128,4096]{1,0:T(8,128)(2,1)} %bitcast.8, bf16[128,4096]{1,0:T(8,128)(2,1)} %bitcast.9, ...), custom_call_target="tpu_custom_call" | custom-call | tf_op jit(solution)/shard_map/conv_backward/pallas_call | solution.py:471
  82.3 1.0 %copy.14 = bf16[1,128,4096]{2,1,0:T(8,128)(2,1)} copy(bf16[1,128,4096]{2,1,0:T(8,128)(2,1)S(1)} %bitcast.6) | data formatting | bytes 2097152
  83.2 1.3 %copy.15 = bf16[1,256,4096]{2,1,0:T(8,128)(2,1)} copy(bf16[1,256,4096]{2,1,0:T(8,128)(2,1)S(1)} %bitcast.5) | data formatting | bytes 4194304
  84.6 0.7 copy.16

commit v4 on v3

--- a/solution.py
+++ b/solution.py
@@ -179,9 +179,9 @@
         part = ref.at[pl.ds(0, ref.shape[0] - ref.shape[0] // n_seq)]
         pltpu.make_async_copy(part, part, send_sem.at[i]).wait()
 
-    exchange(0, lambda to: owners_in, own_got.at[pl.ds(seq, 1)])
     share = taps.at[pl.ds(pl.multiple_of(dp * tile, tile), tile)]
     exchange(2, lambda to: columns(share, to), taps_got.at[dp, seq])
+    exchange(0, lambda to: owners_in, own_got.at[pl.ds(seq, 1)])
     exchange(1, lambda to: columns(conv, to), conv_got.at[seq])
     loads[0].wait()
     loads[1].wait()
@@ -338,14 +338,12 @@
         mr, mi = mixed[:rows], mixed[rows:]
         xr, xi = specs[k, :rows, :lanes], specs[k, rows:, :lanes]
         tr, ti = specs[k, :rows, lanes:], specs[k, rows:, lanes:]
-        made = jnp.concatenate(
-            [
-                jnp.concatenate([tr * mr + ti * mi, xr * mr + xi * mi], axis=1),
-                jnp.concatenate([tr * mi - ti * mr, xr * mi - xi * mr], axis=1),
-            ],
-            axis=0,
+        made = jnp.concatenate([tr * mr + ti * mi, tr * mi - ti * mr], axis=0)
+        turned[k, :, :lanes] = jnp.dot(
+            back_table[k], made.astype(BF16), preferred_element_type=F32
         )
-        turned[k] = jnp.dot(back_table[k], made.astype(BF16), preferred_element_type=F32)
+        cross = jnp.concatenate([xr * mr + xi * mi, xr * mi - xi * mr], axis=0)
+        pair_a[k, :, lanes:] = cross.astype(BF16)
 
     def put_back(q, at, i, found):
         back_time[q, at, :] = found
@@ -383,6 +381,12 @@
     def put_filter(q, at, i, found):
         down = pl.ds(pl.multiple_of((q % per) * rows + i * tile, tile), tile)
         filt_send[q // per, down, :] = found
+
+    @pl.loop(0, n_seq, unroll=16)
+    def _(k):
+        turned[k, :, lanes:] = jnp.dot(
+            back_table[k], pair_a[k, :, lanes:], preferred_element_type=F32
+        )
 
     invert(lanes, put_filter)
 

time: 85.7 us -> 84.2 us (0.982)
  Pallas kernels: 81.6 us -> 80.1 us
    pallas_call x1, Pallas kernels: 81.6 us -> 80.1 us  [per_device(): pl.pallas_call(functools.partial(kernel, n_dp, n_seq), out_shape=(pltpu.V...]
where the time goes in v4:
time: 84.2 us; the launch traced here: 83.7 us
  Pallas kernels  80.1 us (95%)
  local copies, waits for them, and re-layouts  2.99 us (4%)
    pallas_call x1, Pallas kernels, per_device(): pl.pallas_call(functools.partial(kernel, n_dp, n_seq), out_shape=(pltpu.V...  80.1 us
    unnamed x3, local copies, waits for them, and re-layouts  2.99 us

profile of v4, /device:TPU:9, one launch (start us, length us, event | category | flops | bytes accessed | tf_op | source)
XLA Modules:
  0.0 83.7 jit_solution(3908855080371615400)
XLA Ops:
  0.6 80.1 %conv_backward.1 = (bf16[128,4096]{1,0:T(8,128)(2,1)S(1)}, bf16[256,4096]{1,0:T(8,128)(2,1)S(1)}, f32[512,128]{1,0:T(8,128)S(1)}) custom-call(s32[32]{0:T(128)} %order.1, s32[1,128]{1,0:T(1,128)} %owners_in.1, bf16[128,4096]{1,0:T(8,128)(2,1)} %bitcast.7, bf16[128,4096]{1,0:T(8,128)(2,1)} %bitcast.8, bf16[128,4096]{1,0:T(8,128)(2,1)} %bitcast.9, ...), custom_call_target="tpu_custom_call" | custom-call | tf_op jit(solution)/shard_map/conv_backward/pallas_call | solution.py:475
  80.7 1.0 %copy.14 = bf16[1,128,4096]{2,1,0:T(8,128)(2,1)} copy(bf16[1,128,4096]{2,1,0:T(8,128)(2,1)S(1)} %bitcast.6) | data formatting | bytes 2097152
  81.7 1.3 %copy.15 = bf16[1,256,4096]{2,1,0:T(8,128)(2,1)} copy(bf16[1,256,4096]{2,1,0:T(8,128)(2,1)S(1)} %bitcast.5) | data formatting | bytes 4194304
  83.0 0.7 copy.16

commit v5 on v4

--- a/solution.py
+++ b/solution.py
@@ -307,7 +307,7 @@
     loads[2].wait()
     loads[3].wait()
 
-    @pl.loop(0, n_seq, unroll=16)
+    @pl.loop(0, n_seq, unroll=32)
     def _(k):
         both = jnp.dot(table[k], pair_a[k], preferred_element_type=F32)
         specs[k] = both
@@ -332,7 +332,7 @@
     arrived(3, mixed_got)
     transform(lambda q, at, i: mixed_got[place_of[q], at, :], pair_a, 0)
 
-    @pl.loop(0, n_seq, unroll=16)
+    @pl.loop(0, n_seq, unroll=32)
     def _(k):
         mixed = jnp.dot(table[k], pair_a[k, :, :lanes], preferred_element_type=F32)
         mr, mi = mixed[:rows], mixed[rows:]
@@ -350,13 +350,13 @@
 
     invert(0, put_back)
 
-    @pl.loop(0, n_seq, unroll=8)
+    @pl.loop(0, n_seq, unroll=16)
     def _(p):
         found = jnp.dot(slot_of[p], back_time[order[p]], preferred_element_type=F32)
         at = pl.ds(pl.multiple_of(p * slot, slot), slot)
         packed[:, at, :] = found.reshape(n_seq, slot, lanes)
 
-    together = 8
+    together = 16
 
     @pl.loop(0, n_seq // together)
     def _(group):
@@ -382,7 +382,7 @@
         down = pl.ds(pl.multiple_of((q % per) * rows + i * tile, tile), tile)
         filt_send[q // per, down, :] = found
 
-    @pl.loop(0, n_seq, unroll=16)
+    @pl.loop(0, n_seq, unroll=32)
     def _(k):
         turned[k, :, lanes:] = jnp.dot(
             back_table[k], pair_a[k, :, lanes:], preferred_element_type=F32

time: 84.2 us -> 83.3 us (0.989)
  no operation moved by 1% of the time
where the time goes in v5:
time: 83.3 us; the launch traced here: 83.1 us
  Pallas kernels  79.5 us (95%)
  local copies, waits for them, and re-layouts  2.99 us (4%)
    pallas_call x1, Pallas kernels, per_device(): pl.pallas_call(functools.partial(kernel, n_dp, n_seq), out_shape=(pltpu.V...  79.5 us
    unnamed x3, local copies, waits for them, and re-layouts  2.99 us

profile of v5, /device:TPU:9, one launch (start us, length us, event | category | flops | bytes accessed | tf_op | source)
XLA Modules:
  0.0 83.1 jit_solution(16843276242292403842)
XLA Ops:
  0.6 79.5 %conv_backward.1 = (bf16[128,4096]{1,0:T(8,128)(2,1)S(1)}, bf16[256,4096]{1,0:T(8,128)(2,1)S(1)}, f32[512,128]{1,0:T(8,128)S(1)}) custom-call(s32[32]{0:T(128)} %order.1, s32[1,128]{1,0:T(1,128)} %owners_in.1, bf16[128,4096]{1,0:T(8,128)(2,1)} %bitcast.7, bf16[128,4096]{1,0:T(8,128)(2,1)} %bitcast.8, bf16[128,4096]{1,0:T(8,128)(2,1)} %bitcast.9, ...), custom_call_target="tpu_custom_call" | custom-call | tf_op jit(solution)/shard_map/conv_backward/pallas_call | solution.py:475
  80.1 1.0 %copy.14 = bf16[1,128,4096]{2,1,0:T(8,128)(2,1)} copy(bf16[1,128,4096]{2,1,0:T(8,128)(2,1)S(1)} %bitcast.6) | data formatting | bytes 2097152
  81.1 1.3 %copy.15 = bf16[1,256,4096]{2,1,0:T(8,128)(2,1)} copy(bf16[1,256,4096]{2,1,0:T(8,128)(2,1)S(1)} %bitcast.5) | data formatting | bytes 4194304
  82.4 0.7 copy.16
